TPU v7x, 128 devices: a whole 4x4x4 slice. The times are simulated.
128 devices in a mesh: seq: 16 (over z, y), exp: 8 (over x, core).
Axes of the slice: x: 4, y: 4, z: 4, core: 2. Of those that a mesh axis runs over, the one named last changes fastest.
Arguments:
- layer_input: bfloat16 [16384, 2048], P(('seq', 'exp')), may hold values from -24 to 24, as said below
- attn_gain: float32 [2048], replicated, may hold values from 0.1 to 1.9
- query_proj: bfloat16 [2048, 3072], P(None, 'exp'), may hold values from -0.1875 to 0.1875
- latent_proj: bfloat16 [2048, 576], replicated, may hold values from -0.125 to 0.125
- latent_gain: float32 [512], replicated, may hold values from 0.1 to 1.9
- kv_proj: bfloat16 [512, 4096], P(None, 'exp'), may hold values from -0.25 to 0.25
- output_proj: bfloat16 [2048, 2048], P('exp'), may hold values from -3 to 3
- ffn_gain: float32 [2048], replicated, may hold values from 0.1 to 1.9
- router_proj: float32 [2048, 8], replicated, may hold values from -0.0625 to 0.0625
- shared_gate_up: bfloat16 [2048, 2, 2816], P(None, None, 'exp'), may hold values from -0.125 to 0.125
- shared_down: bfloat16 [2816, 2048], P('exp'), may hold values from -0.15625 to 0.15625
- expert_gate_up: bfloat16 [8, 2048, 2816], P('exp'), may hold values from -0.125 to 0.125
- expert_down: bfloat16 [8, 1408, 2048], P('exp'), may hold values from -0.625 to 0.625
- segment_ids: int32 [16384], replicated, may hold values from 0 to 31, as said below
- expert_routes: int32 [16384, 6], P(('seq', 'exp')), may hold values from 0 to 7, all different within a row; in each aligned block of 128 rows (0 to 127, 128 to 255, ...) at most 128 rows name the same one
- out_grad: bfloat16 [16384, 2048], P(('seq', 'exp')), may hold values from -6 to 6
Outputs:
- layer_output: bfloat16 [16384, 2048], P(('seq', 'exp'))
- input_grad: bfloat16 [16384, 2048], P(('seq', 'exp'))
- attn_gain_grad: float32 [2048], replicated
- query_proj_grad: float32 [2048, 3072], P(None, 'exp')
- latent_proj_grad: float32 [2048, 576], replicated
- latent_gain_grad: float32 [512], replicated
- kv_proj_grad: float32 [512, 4096], P(None, 'exp')
- output_proj_grad: float32 [2048, 2048], P('exp')
- ffn_gain_grad: float32 [2048], replicated
- router_grad: float32 [2048, 8], replicated
- shared_gate_up_grad: float32 [2048, 2, 2816], P('seq', None, 'exp')
- shared_down_grad: float32 [2816, 2048], P('exp', 'seq')
- expert_gate_up_grad: float32 [8, 2048, 2816], P('exp', 'seq')
- expert_down_grad: float32 [8, 1408, 2048], P('exp', None, 'seq')
Inputs may be any that keep to these rules, and one draw needn't show every extreme that they name: `layer_input`: the block's input. `segment_ids`: never falls along the tokens; every document lies within one packed sequence of 2048 tokens, and the documents of packed sequence s are numbered 4 s to 4 s + 3. `expert_routes`: each token names 6 different experts; the 128 rows of one device name one expert at most 128 times.
All inputs are finite; a program needn't handle non-finite values.
Results may differ from a plain program's by a relative error of at most 0.029.
Values may be sent and summed in bfloat16 or wider, within the bound.
A program may use at most 256 MiB of HBM per device.

v0:
```python
import functools
import math

import jax
import jax.numpy as jnp
import numpy as np
from jax import lax
from jax.experimental import pallas as pl
from jax.experimental.pallas import tpu as pltpu
from jax.sharding import PartitionSpec as P

NOPE = 128
ROPE = 64
VDIM = 128
LAT = 512
F = 1408
EXPERTS = 8
EPSILON = 1e-06

VM = pltpu.VMEM
f32 = jnp.float32
bf16 = jnp.bfloat16


class Sems:
    def __init__(self, send, recv):
        self.send, self.recv, self.used, self.sent = send, recv, 0, []

    def start(self, src, dst, peer):
        copy = pltpu.make_async_remote_copy(
            src_ref=src,
            dst_ref=dst,
            send_sem=self.send.at[self.used],
            recv_sem=self.recv.at[self.used],
            device_id=peer,
            device_id_type=pl.DeviceIdType.MESH,
        )
        copy.start()
        self.used += 1
        self.sent.append(copy)
        return copy

    def finish(self):
        for copy in self.sent:
            copy.wait_send()


class Place:
    def __init__(self):
        me, spot = lax.axis_index("exp"), lax.axis_index("seq")
        self.me = me
        self.chip, self.core = me // 2, me % 2
        self.z, self.y = spot // 4, spot % 4
        self.sibling = {"exp": self.chip * 2 + 1 - self.core}
        self.across = [lambda i: {"exp": i * 2 + self.core}, lambda i: {"seq": self.z * 4 + i}, lambda i: {"seq": i * 4 + self.y}]
        self.along = [self.chip, self.y, self.z]

    def hop(self, axis, distance):
        return self.across[axis](lax.rem(self.along[axis] + distance, 4))


def announce(peers):
    barrier = pltpu.get_barrier_semaphore()
    for peer in peers:
        pl.semaphore_signal(barrier, inc=1, device_id=peer, device_id_type=pl.DeviceIdType.MESH)
    return len(peers)


def meet(count):
    pl.semaphore_wait(pltpu.get_barrier_semaphore(), count)


def greet(peers):
    meet(announce(peers))


def together(*streams):
    streams = list(streams)
    while streams:
        for stream in list(streams):
            try:
                next(stream)
            except StopIteration:
                streams.remove(stream)


def gather_stream(sems, at, src, out, rows, local, arrived=None, stride=None, offset=0):
    half = rows // 2
    stride = stride or rows
    right, left = at.hop(0, 1), at.hop(0, 3)
    me = at.me
    near_right = lax.rem(at.chip + 1, 4) * 2 + at.core
    near_left = lax.rem(at.chip + 3, 4) * 2 + at.core
    far = lax.rem(at.chip + 2, 4) * 2 + at.core

    def part(owner, h):
        return out.at[pl.ds(pl.multiple_of(owner * stride + offset + h * half, half), half)]

    def own(h):
        return src.at[pl.ds(h * half, half)]

    ra = sems.start(own(0), part(me, 0), right)
    lb = sems.start(own(1), part(me, 1), left)
    rb = sems.start(own(1), part(me, 1), right)
    la = sems.start(own(0), part(me, 0), left)
    sib = [sems.start(src, out.at[pl.ds(pl.multiple_of(me * stride + offset, rows), rows)], at.sibling)]
    mine = pltpu.make_async_copy(src, out.at[pl.ds(pl.multiple_of(me * stride + offset, rows), rows)], local)
    mine.start()
    if arrived is None:
        yield
    else:
        mine.wait()
        sib[0].wait_recv()
        arrived(0)
    ra.wait_recv()
    far_a = sems.start(part(near_left, 0), part(near_left, 0), right)
    sib.append(sems.start(part(near_left, 0), part(near_left, 0), at.sibling))
    lb.wait_recv()
    far_b = sems.start(part(near_right, 1), part(near_right, 1), left)
    sib.append(sems.start(part(near_right, 1), part(near_right, 1), at.sibling))
    if arrived is None:
        yield
    rb.wait_recv()
    sib.append(sems.start(part(near_left, 1), part(near_left, 1), at.sibling))
    la.wait_recv()
    sib.append(sems.start(part(near_right, 0), part(near_right, 0), at.sibling))
    yield
    if arrived is not None:
        sib[1].wait_recv()
        sib[3].wait_recv()
        arrived(3)
    far_a.wait_recv()
    sib.append(sems.start(part(far, 0), part(far, 0), at.sibling))
    far_b.wait_recv()
    sib.append(sems.start(part(far, 1), part(far, 1), at.sibling))
    yield
    if arrived is None:
        mine.wait()
        for copy in sib:
            copy.wait_recv()
    else:
        sib[2].wait_recv()
        sib[4].wait_recv()
        arrived(1)
        yield
        sib[5].wait_recv()
        sib[6].wait_recv()
        arrived(2)


def scatter_stream(sems, at, src, pair, hop, last, rows, done, ready=None, stride=None, offset=0):
    half = rows // 2
    stride = stride or rows
    right, left = at.hop(0, 1), at.hop(0, 3)
    order = (2, 1, 3, 0)
    sib = []

    def offer(dist):
        if ready is not None:
            ready(dist)
        owner = lax.rem(at.chip + dist, 4) * 2 + 1 - at.core
        sib.append(sems.start(src.at[pl.ds(pl.multiple_of(owner * stride + offset, rows), rows)], pair.at[dist], at.sibling))

    def fold(i):
        sib[i].wait_recv()
        owner = lax.rem(at.chip + order[i], 4) * 2 + at.core
        mine = src[pl.ds(pl.multiple_of(owner * stride + offset, rows), rows)]
        pair[order[i]] = (pair[order[i]].astype(f32) + mine.astype(f32)).astype(bf16)

    def add(ref, other):
        ref[...] = (ref[...].astype(f32) + other[...].astype(f32)).astype(bf16)

    first, second = pl.ds(0, half), pl.ds(half, half)
    offer(2)
    if ready is not None:
        yield
    offer(1)
    if ready is None:
        offer(3)
        offer(0)
        yield
    fold(0)
    far_a = sems.start(pair.at[2, first], hop.at[0], right)
    far_b = sems.start(pair.at[2, second], hop.at[1], left)
    yield
    if ready is not None:
        offer(3)
    fold(1)
    dir_b = sems.start(pair.at[1, second], last.at[0], right)
    fold(2)
    dir_a = sems.start(pair.at[3, first], last.at[1], left)
    yield
    far_a.wait_recv()
    add(pair.at[1, first], hop.at[0])
    acc_a = sems.start(pair.at[1, first], last.at[2], right)
    far_b.wait_recv()
    add(pair.at[3, second], hop.at[1])
    acc_b = sems.start(pair.at[3, second], last.at[3], left)
    if ready is not None:
        offer(0)
    yield
    sib[3].wait_recv()
    dir_b.wait_recv()
    dir_a.wait_recv()
    acc_a.wait_recv()
    acc_b.wait_recv()
    for h, ends in ((0, (1, 2)), (1, (0, 3))):
        mine = src[pl.ds(pl.multiple_of(at.me * stride + offset + h * half, half), half)].astype(f32)
        total = mine + pair[0, pl.ds(h * half, half)].astype(f32)
        done(h, total + last[ends[0]].astype(f32) + last[ends[1]].astype(f32))


def scatter_scratch(rows, cols):
    return [
        pltpu.VMEM((4, rows, cols), bf16),
        pltpu.VMEM((2, rows // 2, cols), bf16),
        pltpu.VMEM((4, rows // 2, cols), bf16),
    ]


def ring_sum(sems, at, axis, block, hop, last):
    right, left = at.hop(axis, 1), at.hop(axis, 3)
    to = [lax.rem(at.along[axis] + d, 4) for d in range(4)]

    def add(ref, other):
        ref[...] = (ref[...].astype(f32) + other[...].astype(f32)).astype(bf16)

    far_a = sems.start(block(to[2], 0), hop.at[0], right)
    far_b = sems.start(block(to[2], 1), hop.at[1], left)
    dir_b = sems.start(block(to[1], 1), last.at[0], right)
    dir_a = sems.start(block(to[3], 0), last.at[1], left)
    yield
    far_a.wait_recv()
    add(block(to[1], 0), hop.at[0])
    acc_a = sems.start(block(to[1], 0), last.at[2], right)
    far_b.wait_recv()
    add(block(to[3], 1), hop.at[1])
    acc_b = sems.start(block(to[3], 1), last.at[3], left)
    yield
    dir_b.wait_recv()
    dir_a.wait_recv()
    acc_a.wait_recv()
    acc_b.wait_recv()
    for part, (one, two) in ((0, (1, 2)), (1, (0, 3))):
        ref = block(to[0], part)
        ref[...] = (ref[...].astype(f32) + last[one].astype(f32) + last[two].astype(f32)).astype(bf16)


def ring_gather(sems, at, axis, block):
    right, left = at.hop(axis, 1), at.hop(axis, 3)
    to = [lax.rem(at.along[axis] + d, 4) for d in range(4)]
    ra = sems.start(block(to[0], 0), block(to[0], 0), right)
    lb = sems.start(block(to[0], 1), block(to[0], 1), left)
    rb = sems.start(block(to[0], 1), block(to[0], 1), right)
    la = sems.start(block(to[0], 0), block(to[0], 0), left)
    yield
    ra.wait_recv()
    fa = sems.start(block(to[3], 0), block(to[3], 0), right)
    lb.wait_recv()
    fb = sems.start(block(to[1], 1), block(to[1], 1), left)
    yield
    for copy in (rb, la, fa, fb):
        copy.wait_recv()


def seq_stream(sems, at, work, out, scratch, axes):
    hop, last, narrow_in = scratch
    one, two = at.along[axes[0]], at.along[axes[1]]
    own = one * 4 + two

    def wide(ref):
        return lambda i, h: ref.at[pl.ds(i * 4 + 2 * h, 2)]

    yield from ring_sum(sems, at, axes[0], wide(work), hop, last)
    copies = [sems.start(work.at[one * 4 + lax.rem(two + d, 4)], narrow_in.at[d - 1], at.hop(axes[1], d)) for d in (1, 2, 3)]
    yield
    for copy in copies:
        copy.wait_recv()
    total = work[own].astype(f32) + narrow_in[0].astype(f32)
    out[own] = (total + (narrow_in[1].astype(f32) + narrow_in[2].astype(f32))).astype(bf16)
    copies = [sems.start(out.at[own], out.at[own], at.hop(axes[1], d)) for d in (1, 2, 3)]
    yield
    for copy in copies:
        copy.wait_recv()
    yield from ring_gather(sems, at, axes[0], wide(out))


def seq_scatter(sems, at, work, out, scratch, axes):
    hop, last, narrow_in = scratch
    one, two = at.along[axes[0]], at.along[axes[1]]
    yield from ring_sum(sems, at, axes[0], lambda i, h: work.at[pl.ds(i * 4 + 2 * h, 2)], hop, last)
    copies = [sems.start(work.at[one * 4 + lax.rem(two + d, 4)], narrow_in.at[d - 1], at.hop(axes[1], d)) for d in (1, 2, 3)]
    yield
    for copy in copies:
        copy.wait_recv()
    total = work[one * 4 + two].astype(f32) + narrow_in[0].astype(f32)
    out[...] = (total + (narrow_in[1].astype(f32) + narrow_in[2].astype(f32))).astype(bf16)


def seq_scratch(rows, cols):
    return [
        pltpu.VMEM((2, 2, rows, cols), bf16),
        pltpu.VMEM((4, 2, rows, cols), bf16),
        pltpu.VMEM((3, rows, cols), bf16),
    ]


def seq_direct(sems, at, work, out, wide_in, narrow_in):
    y, z = at.y, at.z
    copies = [sems.start(work.at[pl.ds(lax.rem(y + d, 4) * 4, 4)], wide_in.at[d - 1], at.hop(1, d)) for d in (1, 2, 3)]
    yield
    for copy in copies:
        copy.wait_recv()
    mine = pl.ds(y * 4, 4)
    work[mine] = (
        work[mine].astype(f32) + wide_in[0].astype(f32) + (wide_in[1].astype(f32) + wide_in[2].astype(f32))
    ).astype(bf16)
    copies = [sems.start(work.at[y * 4 + lax.rem(z + d, 4)], narrow_in.at[d - 1], at.hop(2, d)) for d in (1, 2, 3)]
    yield
    for copy in copies:
        copy.wait_recv()
    own = y * 4 + z
    out[own] = (
        work[own].astype(f32) + narrow_in[0].astype(f32) + (narrow_in[1].astype(f32) + narrow_in[2].astype(f32))
    ).astype(bf16)
    copies = [sems.start(out.at[own], out.at[own], at.hop(2, d)) for d in (1, 2, 3)]
    yield
    for copy in copies:
        copy.wait_recv()
    copies = [sems.start(out.at[mine], out.at[mine], at.hop(1, d)) for d in (1, 2, 3)]
    yield
    for copy in copies:
        copy.wait_recv()


def small_stream(sems, at, slots, out):
    stages = [(at.core, 2, lambda d: at.sibling)] + [
        (at.along[axis], 4, functools.partial(at.hop, axis)) for axis in range(3)
    ]
    for stage, (place, count, name) in enumerate(stages):
        slots[stage, place] = out[...].astype(bf16)
        copies = [sems.start(slots.at[stage, place], slots.at[stage, place], name(d)) for d in range(1, count)]
        yield
        for copy in copies:
            copy.wait_recv()
        total = slots[stage, 0].astype(f32)
        for i in range(1, count):
            total = total + slots[stage, i].astype(f32)
        out[...] = total


def swapped(tensor):
    lane = lax.broadcasted_iota(jnp.int32, tensor.shape, 1)
    return jnp.where(lane % 64 < 32, pltpu.roll(tensor, 96, 1), pltpu.roll(tensor, 32, 1))


PAD = 384
EARLY = 768
ROW_STEP = 256


def dot_nn(a, b):
    return lax.dot_general(a, b, (((1,), (0,)), ((), ())), preferred_element_type=f32)


def dot_nt(a, b):
    return lax.dot_general(a, b, (((1,), (1,)), ((), ())), preferred_element_type=f32)


def dot_tn(a, b):
    return lax.dot_general(a, b, (((0,), (0,)), ((), ())), preferred_element_type=f32)


def row_block(index):
    return pl.ds(pl.multiple_of(index * ROW_STEP, ROW_STEP), ROW_STEP)


def router_pieces(router):
    high = router.astype(bf16).astype(f32)
    middle_part = (router - high).astype(bf16).astype(f32)
    low = router - high - middle_part
    fill = jnp.zeros((128 - 3 * EXPERTS, router.shape[1]), f32)
    return jnp.concatenate([high, middle_part, low, fill], axis=0).astype(bf16)


def mlp_kernel(
    own_mid, own_grad, pair_s_h, pair_e_h, down_s_h, down_e_h, grad_h, router, hot,
    terms_h, act_h, dpre_h, logit, router_out, early,
    mid, grad, pair_s, pair_e, down_s, down_e, act, dpre, pieces, stage, work0, work1, r0, r1, r2, s0, s1, s2, load, store, keep, send, recv, local,
):
    at = Place()
    sems = Sems(send, recv)
    rows, width = mid.shape
    shared = down_s.shape[0]
    expert = lax.axis_index("exp")
    sources = [(pair_e_h, pair_e), (pair_s_h, pair_s), (down_s_h, down_s), (down_e_h, down_e)]
    loads = [pltpu.make_async_copy(src, dst, load.at[i]) for i, (src, dst) in enumerate(sources)]
    sent = own_grad.shape[0] // 2
    for owner in range(8):
        here = (grad_h.at[pl.ds(owner * sent, sent)], grad.at[pl.ds(owner * 2 * sent, sent)])
        loads.append(pltpu.make_async_copy(*here, load.at[len(loads)]))
    for c in loads:
        c.start()
    count = announce(
        [at.hop(0, 1), at.hop(0, 3), at.sibling] + [at.hop(axis, d) for axis in (1, 2) for d in (1, 2, 3)]
    )
    pieces[...] = router_pieces(router[...])
    meet(count)
    lane = lax.broadcasted_iota(jnp.int32, (ROW_STEP, 128), 1)
    own_lane = lane == expert

    def gates(r):
        raw = dot_nt(mid[r], pieces[...])
        raw = raw + (pltpu.roll(raw, 128 - EXPERTS, 1) + pltpu.roll(raw, 128 - 2 * EXPERTS, 1))
        raw = jnp.where(lane < EXPERTS, raw, -1e30)
        raw = jnp.exp(raw - jnp.max(raw, axis=1, keepdims=True))
        probs = raw / jnp.sum(raw, axis=1, keepdims=True)
        own = jnp.sum(jnp.where(own_lane, probs * hot[r].astype(f32), 0.0), axis=1, keepdims=True)
        return own, probs

    tiles = [(pair_e, start, min(512, F - start)) for start in range(0, F, 512)]

    def before_activation(dist):
        r = row_block(lax.rem(at.chip + dist, 4))
        if dist == 0:
            loads[0].wait()
        for _, start, size in tiles:
            dpre[r, start : start + size] = dot_nn(mid[r], pair_e[:, start : start + size]).astype(bf16)
            up = dot_nn(mid[r], pair_e[:, F + start : F + start + size])
            dpre[r, F + start : F + start + size] = up.astype(bf16)
        if dist == 0:
            loads[1].wait()
        dpre[r, 2 * F : 2 * F + shared] = dot_nt(mid[r], pair_s[:shared]).astype(bf16)
        dpre[r, 2 * F + PAD : 2 * F + PAD + shared] = dot_nt(mid[r], pair_s[shared:]).astype(bf16)

    def piece(r, dact, act_at, gate_at, up_at, own):
        size = dact.shape[1]
        gate, up = dpre[r, gate_at : gate_at + size].astype(f32), dpre[r, up_at : up_at + size].astype(f32)
        logistic = 1.0 / (1.0 + jnp.exp(-gate))
        passed = gate * logistic
        out = passed * up
        total = None
        if own is not None:
            total = jnp.sum(out * dact, axis=1, keepdims=True)
            out = out * own
            dact = dact * own
        act[r, act_at : act_at + size] = out.astype(bf16)
        slope = logistic + passed * (1.0 - logistic)
        dpre[r, gate_at : gate_at + size] = (dact * up * slope).astype(bf16)
        dpre[r, up_at : up_at + size] = (dact * passed).astype(bf16)
        return total

    mids = gather_stream(sems, at, own_mid, mid, own_mid.shape[0], local.at[0], before_activation)
    grads = gather_stream(sems, at, own_grad.at[pl.ds(sent, sent)], grad, sent, local.at[1], None, 2 * sent, sent)
    next(mids)
    next(grads)
    next(mids)
    next(mids)
    next(grads)
    together(mids)
    together(grads)
    for c in loads[2:]:
        c.wait()

    @pl.loop(0, rows // ROW_STEP)
    def _(index):
        r = row_block(index)
        piece(r, dot_nt(grad[r], down_s[...]), F, 2 * F, 2 * F + PAD, None)
        own, probs = gates(r)
        total = 0.0
        for _, start, size in tiles:
            total = total + piece(r, dot_nt(grad[r], down_e[start : start + size]), start, start, F + start, own)
        logit[r] = ((own * total) * (jnp.where(own_lane, 1.0, 0.0) - probs)).astype(bf16)

    keeps = [pltpu.make_async_copy(act, act_h, keep.at[0]), pltpu.make_async_copy(dpre, dpre_h, keep.at[1])]
    for c in keeps:
        c.start()

    half = width // 2
    slots = half // 128
    early_rows = EARLY // 2
    for work, start, axis in ((work0, 0, 1), (work1, early_rows, 2)):
        for part in range(2):
            value = dot_tn(act[:, start : start + early_rows], grad[:, part * half : (part + 1) * half]).astype(bf16)
            for s in range(slots):
                z, y = divmod(part * slots + s, 4)
                work[y * 4 + z if axis == 1 else z * 4 + y] = value[:, s * 128 : (s + 1) * 128]
    sums = [
        seq_scatter(sems, at, work0, early.at[pl.ds(0, early_rows)], (r0, r1, r2), (1, 2)),
        seq_scatter(sems, at, work1, early.at[pl.ds(early_rows, early_rows)], (s0, s1, s2), (2, 1)),
    ]
    for stream in sums:
        next(stream)
    jobs = []
    for start in range(0, 2 * F, 512):
        size = min(512, 2 * F - start)
        jobs.append((mid, dpre, start, size, start, True))
    for start in range(EARLY, F, 512):
        size = min(512, F - start)
        jobs.append((grad, act, start, size, 2 * F + start - EARLY, False))
    for index, (left, right, start) in enumerate(((mid, dpre, 2 * F), (mid, dpre, 2 * F + PAD), (grad, act, F))):
        jobs.append((left, right, start, shared, 3 * F - EARLY + index * shared, False))

    def flush(part, spot, size):
        return pltpu.make_async_copy(
            stage.at[part, :, pl.ds(0, size)], terms_h.at[pl.ds(part * slots, slots), pl.ds(spot, size)], store.at[part]
        )

    before = None
    for number, (left, right, start, size, spot, by_column) in enumerate(jobs):
        for part in range(2):
            if before is not None:
                flush(part, *before).wait()
            wide = left[:, part * half : (part + 1) * half]
            if by_column:
                value = dot_tn(wide, right[:, start : start + size]).astype(bf16)
                for s in range(slots):
                    for c in range(size // 128):
                        stage[part, s, c * 128 : (c + 1) * 128] = value[s * 128 : (s + 1) * 128, c * 128 : (c + 1) * 128]
            else:
                value = dot_tn(right[:, start : start + size], wide).astype(bf16)
                for s in range(slots):
                    stage[part, s, :size] = value[:, s * 128 : (s + 1) * 128]
            flush(part, spot, size).start()
        before = (spot, size)
        if number in (3, 7):
            for stream in sums:
                next(stream)
    router_out[...] = dot_tn(logit[...], mid[...])[:EXPERTS]
    for part in range(2):
        flush(part, *before).wait()
    for c in keeps:
        c.wait()
    together(*sums)
    sems.finish()


def mlp(own_mid, own_grad, pair_s, pair_e, down_s, down_e, grad_half, router, hot):
    rows, width = 8 * own_mid.shape[0], own_mid.shape[1]
    shared = down_s.shape[0]
    whole = pl.BlockSpec(memory_space=VM)
    held = pl.BlockSpec(memory_space=pl.ANY)
    act_shape, dpre_shape = (rows, F + PAD), (rows, 2 * (F + PAD))
    return pl.pallas_call(
        mlp_kernel,
        out_shape=[
            jax.ShapeDtypeStruct((width // 128, 3 * (F + shared) - EARLY, 128), bf16),
            jax.ShapeDtypeStruct(act_shape, bf16),
            jax.ShapeDtypeStruct(dpre_shape, bf16),
            jax.ShapeDtypeStruct((rows, 128), bf16),
            jax.ShapeDtypeStruct((EXPERTS, width), f32),
            jax.ShapeDtypeStruct((EARLY, 128), bf16),
        ],
        in_specs=[whole] * 2 + [held] * 5 + [whole] * 2,
        out_specs=[held, held, held, whole, whole, whole],
        scratch_shapes=[
            pltpu.VMEM((rows, width), bf16), pltpu.VMEM((rows, width), bf16),
            pltpu.VMEM(pair_s.shape, bf16), pltpu.VMEM(pair_e.shape, bf16),
            pltpu.VMEM(down_s.shape, bf16), pltpu.VMEM(down_e.shape, bf16),
            pltpu.VMEM(act_shape, bf16), pltpu.VMEM(dpre_shape, bf16),
            pltpu.VMEM((128, width), bf16), pltpu.VMEM((2, width // 256, 512, 128), bf16),
            pltpu.VMEM((width // 128, EARLY // 2, 128), bf16), pltpu.VMEM((width // 128, EARLY // 2, 128), bf16),
            *seq_scratch(EARLY // 2, 128), *seq_scratch(EARLY // 2, 128),
            pltpu.SemaphoreType.DMA((12,)), pltpu.SemaphoreType.DMA((2,)), pltpu.SemaphoreType.DMA((2,)),
            pltpu.SemaphoreType.DMA((44,)), pltpu.SemaphoreType.DMA((44,)), pltpu.SemaphoreType.DMA((2,)),
        ],
        compiler_params=pltpu.CompilerParams(collective_id=5, has_side_effects=True, vmem_limit_bytes=62 << 20),
        cost_estimate=pl.CostEstimate(flops=12 * rows * width * (F + shared), bytes_accessed=60 << 20, transcendentals=rows * F),
        name="mlp",
    )(own_mid, own_grad, pair_s, pair_e, down_s, down_e, grad_half, router, hot)


def turn_kernel(
    dpre_h, act_h, pair_s_h, pair_e_h, down_s_h, down_e_h, logit, router, residual, gain, upstream,
    residual_grad, gain_term, grad_all, moe_h,
    moe_part, dpre, act, pair_s, pair_e, down_s, down_e, part, pieces, own_grad, p0, p1, p2, o0, o1, o2, load, send, recv, local,
):
    at = Place()
    sems = Sems(send, recv)
    rows = residual.shape[0]
    half = rows // 2
    shared = down_s.shape[0]
    sources = [
        (pair_e_h.at[:, pl.ds(0, F)], pair_e.at[:, pl.ds(0, F)]),
        (pair_e_h.at[:, pl.ds(F, F)], pair_e.at[:, pl.ds(F, F)]), (pair_s_h, pair_s),
        (act_h, act), (down_e_h, down_e), (down_s_h, down_s),
    ]
    blocks = [row_block(lax.rem(at.chip + dist, 4)) for dist in (2, 1, 3, 0)]
    sources = [(dpre_h.at[blocks[0]], dpre.at[blocks[0]])] + sources
    sources[4:4] = [(dpre_h.at[r], dpre.at[r]) for r in blocks[1:]]
    loads = [pltpu.make_async_copy(src, dst, load.at[i]) for i, (src, dst) in enumerate(sources)]
    for c in loads:
        c.start()
    count = announce([at.hop(0, 1), at.hop(0, 3), at.sibling])
    gain_term[...] = jnp.zeros_like(gain_term)
    pieces[...] = router_pieces(router[...])
    loads[0].wait()

    def ready(dist):
        r = row_block(lax.rem(at.chip + dist, 4))
        if dist == 2:
            loads[1].wait()
        else:
            loads[{1: 4, 3: 5, 0: 6}[dist]].wait()
        total = dot_nt(dpre[r, :F], pair_e[:, :F])
        if dist == 2:
            loads[2].wait()
        total = total + dot_nt(dpre[r, F : 2 * F], pair_e[:, F:])
        if dist == 2:
            loads[3].wait()
        total = total + dot_nn(dpre[r, 2 * F : 2 * F + shared], pair_s[:shared])
        total = total + dot_nn(dpre[r, 2 * F + PAD : 2 * F + PAD + shared], pair_s[shared:])
        part[r] = (total + dot_nn(logit[r], pieces[...])).astype(bf16)
        if dist == 2:
            meet(count)

    def done_from(first):
        def done(h, total):
            r = slice(first + h * (half // 2), first + (h + 1) * (half // 2))
            x = residual[r]
            inverse = lax.rsqrt(jnp.mean(x * x, axis=1, keepdims=True) + EPSILON)
            gain_term[...] += jnp.sum(total * x * inverse, axis=0, keepdims=True)
            s = total * gain[...]
            inner = jnp.mean(s * x, axis=1, keepdims=True)
            grad = upstream[r].astype(f32) + (inverse * s - x * (inverse * inverse * inverse) * inner)
            residual_grad[r] = grad
            own_grad[r] = grad.astype(bf16)

        return done

    def moe(index):
        r = pl.ds(index * ROW_STEP, ROW_STEP)
        moe_part[r] = (dot_nn(act[r, :F], down_e[...]) + dot_nn(act[r, F : F + shared], down_s[...])).astype(bf16)

    ones = scatter_stream(sems, at, part, p0, p1, p2, half, done_from(0), ready, rows, 0)
    twos = scatter_stream(sems, at, part, o0, o1, o2, half, done_from(half), lambda dist: None, rows, half)
    for _ in range(4):
        next(ones)
        next(twos)
    together(ones)
    first = gather_stream(sems, at, own_grad.at[pl.ds(0, half)], grad_all, half, local.at[0], None, rows, 0)
    next(first)
    together(twos)
    second = gather_stream(sems, at, own_grad.at[pl.ds(half, half)], grad_all, half, local.at[1], None, rows, half)
    next(second)
    for c in loads[7:]:
        c.wait()
    for index in range(4):
        moe(index)
        next(first, None)
        next(second, None)
    keep = pltpu.make_async_copy(moe_part, moe_h, load.at[0])
    keep.start()
    together(first, second)
    keep.wait()
    sems.finish()


def turn(dpre, act, pair_s, pair_e, down_s, down_e, logit, router, residual, gain, upstream):
    whole = pl.BlockSpec(memory_space=VM)
    held = pl.BlockSpec(memory_space=pl.ANY)
    rows, width = residual.shape
    return pl.pallas_call(
        turn_kernel,
        out_shape=[
            jax.ShapeDtypeStruct((rows, width), f32),
            jax.ShapeDtypeStruct((1, width), f32),
            jax.ShapeDtypeStruct((8 * rows, width), bf16),
            jax.ShapeDtypeStruct((8 * rows, width), bf16),
        ],
        in_specs=[held] * 6 + [whole] * 5,
        out_specs=[whole] * 3 + [held],
        scratch_shapes=[
            pltpu.VMEM((8 * rows, width), bf16),
            pltpu.VMEM(dpre.shape, bf16), pltpu.VMEM(act.shape, bf16),
            pltpu.VMEM(pair_s.shape, bf16), pltpu.VMEM(pair_e.shape, bf16),
            pltpu.VMEM(down_s.shape, bf16), pltpu.VMEM(down_e.shape, bf16),
            pltpu.VMEM((8 * rows, width), bf16),
            pltpu.VMEM((128, width), bf16),
            pltpu.VMEM((rows, width), bf16),
            *scatter_scratch(rows // 2, width),
            *scatter_scratch(rows // 2, width),
            pltpu.SemaphoreType.DMA((10,)),
            pltpu.SemaphoreType.DMA((46,)),
            pltpu.SemaphoreType.DMA((46,)),
            pltpu.SemaphoreType.DMA((2,)),
        ],
        compiler_params=pltpu.CompilerParams(collective_id=2, has_side_effects=True, vmem_limit_bytes=62 << 20),
        name="turn",
    )(dpre, act, pair_s, pair_e, down_s, down_e, logit, router, residual, gain, upstream)


SPAN = LAT + 2 * ROPE
ATT = 256
SCALE = (NOPE + ROPE) ** (-0.5)
LOG2E = 1.4426950408889634


def segments(segs, count):
    spot = lax.axis_index("seq")
    own = segs[:, pl.ds(pl.multiple_of(spot * count, count), count)].astype(f32)
    before = segs[:, pl.ds(pl.multiple_of(jnp.maximum(spot - 1, 0) * count, count), count)].astype(f32)
    before = jnp.where(lax.rem(spot, 2) == 1, before, -1.0)
    column = jnp.transpose(jnp.broadcast_to(own, (128, count)))[:, :1]
    return column, jnp.concatenate([before, own], axis=1)


def attend_back_kernel(
    segs, wo_h, grad_h, moe_h, packed_h, keys_h, q_h, heads_h, lse_h, residual_h, kv_proj_h, cosine_h, sine_h,
    dq, key_own, prev_out, kvo, layer_out,
    key_prev, head_grad, dkey, dvalue, drope, dpacked, dquery, cosine, sine,
    wo, grad, moe_part, packed, keys_all, q, heads, lse, residual, kv_proj,
    p0, p1, p2, k0, k1, k2, send, recv, load,
):
    at = Place()
    sems = Sems(send, recv)
    rows = q.shape[0]
    prev = packed.shape[0] - rows
    block = pl.ds(pl.multiple_of(lax.rem(at.y, 2) * rows, rows), rows)
    sources = (
        (wo_h, wo), (grad_h, grad), (moe_h, moe_part), (packed_h, packed), (keys_h, keys_all), (q_h, q),
        (heads_h, heads), (lse_h, lse), (residual_h, residual), (kv_proj_h, kv_proj),
        (cosine_h.at[block], cosine), (sine_h.at[block], sine),
    )
    loads = [pltpu.make_async_copy(src, dst, load.at[i]) for i, (src, dst) in enumerate(sources)]
    for c in loads:
        c.start()
    count = announce([at.hop(0, 1), at.hop(0, 3), at.sibling])
    own_rows = residual.shape[0]

    def done(h, total):
        r = slice(h * (own_rows // 2), (h + 1) * (own_rows // 2))
        layer_out[r] = (residual[r] + total).astype(bf16)

    def keep_prev(h, total):
        prev_out[h * (own_rows // 2) : (h + 1) * (own_rows // 2)] = total.astype(bf16)

    step = 256
    loads[0].wait()
    loads[1].wait()
    for i in range(rows // step):
        r = pl.ds(i * step, step)
        head_grad[r] = dot_nt(grad[r], wo[...]).astype(bf16)
    meet(count)
    loads[2].wait()
    moe = scatter_stream(sems, at, moe_part, p0, p1, p2, own_rows, done)
    next(moe)
    for c in loads[3:]:
        c.wait()
    qseg, kseg = segments(segs, rows)

    def block_back(head, start, size, lo, hi, diagonal):
        r = slice(start, start + size)
        lane = lax.broadcasted_iota(jnp.int32, (size, 2 * ROPE), 1)
        rope = jnp.where(lane // ROPE == head, q[r, 2 * NOPE :], jnp.zeros((), bf16))
        query = jnp.concatenate([q[r, head * NOPE : (head + 1) * NOPE], rope], axis=1)
        keys = jnp.concatenate([packed[lo:hi, head * 2 * NOPE : head * 2 * NOPE + NOPE], keys_all[lo:hi, LAT:]], axis=1)
        scores = dot_nt(query, keys)
        allowed = qseg[r] == kseg[:, lo:hi]
        if diagonal:
            ahead = lax.broadcasted_iota(jnp.int32, scores.shape, 1) - lax.broadcasted_iota(jnp.int32, scores.shape, 0)
            allowed = allowed & (ahead <= start)
        p = jnp.exp2(jnp.where(allowed, scores * (SCALE * LOG2E) - lse[head, r], -1e30))
        upstream = head_grad[r, head * VDIM : (head + 1) * VDIM]
        out = heads[r, head * VDIM : (head + 1) * VDIM]
        inner = jnp.sum(upstream.astype(f32) * out.astype(f32), axis=1, keepdims=True)
        d = dot_nt(upstream, packed[lo:hi, head * 2 * NOPE + NOPE : (head + 1) * 2 * NOPE])
        ds = (p * (d - inner)).astype(bf16)
        dkey[lo:hi] += dot_tn(ds, query)
        dvalue[lo:hi] += dot_tn(p.astype(bf16), upstream)
        return dot_nn(ds, keys)

    def keys_back(head, lo, hi):
        dpacked[lo:hi, head * 2 * NOPE : head * 2 * NOPE + NOPE] = (dkey[lo:hi, :NOPE] * SCALE).astype(bf16)
        dpacked[lo:hi, head * 2 * NOPE + NOPE : (head + 1) * 2 * NOPE] = dvalue[lo:hi].astype(bf16)
        if head == 0:
            drope[lo:hi] = dkey[lo:hi, NOPE:]
        else:
            drope[lo:hi] += dkey[lo:hi, NOPE:]

    def latent_back(ref, lo):
        for start in range(0, rows, 512):
            r, to = slice(lo + start, lo + start + 512), slice(start, start + 512)
            ref[to, :LAT] = dot_nt(dpacked[r], kv_proj[...]).astype(bf16)
            rope = drope[r]
            ref[to, LAT:] = ((rope + pltpu.roll(rope, ROPE, 1)) * SCALE).astype(bf16)

    wide_step = 512
    for head in range(2):
        dkey[...] = jnp.zeros_like(dkey)
        dvalue[...] = jnp.zeros_like(dvalue)
        for start in range(0, rows, wide_step):
            dquery[head, start : start + wide_step] = block_back(head, start, wide_step, 0, prev, False)
            if (head, start) != (1, wide_step):
                next(moe, None)
        keys_back(head, 0, prev)
    latent_back(key_prev, 0)
    prevs = scatter_stream(sems, at, key_prev, k0, k1, k2, own_rows, keep_prev)
    next(prevs)
    for head in range(2):
        dkey[prev:] = jnp.zeros_like(dkey[prev:])
        dvalue[prev:] = jnp.zeros_like(dvalue[prev:])
        for i in range(rows // ATT):
            r = slice(ATT * i, ATT * (i + 1))
            total = dquery[head, r] + block_back(head, ATT * i, ATT, prev, prev + ATT * (i + 1), True)
            dquery[head, r] = total * SCALE
            if head == 1:
                lane = lax.broadcasted_iota(jnp.int32, (ATT, 2 * ROPE), 1)
                rope = jnp.where(lane < ROPE, dquery[0, r, NOPE:], dquery[1, r, NOPE:])
                rope = rope * cosine[r] - swapped(rope) * sine[r]
                turned = pltpu.roll(dquery[1, r, :NOPE], ROPE, 1)
                dq[r, :NOPE] = dquery[0, r, :NOPE].astype(bf16)
                dq[r, NOPE : 2 * NOPE] = jnp.where(lane < ROPE, rope, turned).astype(bf16)
                dq[r, 2 * NOPE :] = jnp.where(lane < ROPE, turned, rope).astype(bf16)
            if (head, i) in ((0, 2), (1, 0), (1, 2)):
                next(prevs, None)
            if (head, i) == (1, 1):
                together(moe)
        keys_back(head, prev, prev + rows)
    latent_back(key_own, prev)
    spots, wide = kvo.shape[0], kvo.shape[2]
    kv = dot_tn(keys_all[:, :LAT], dpacked[...]).astype(bf16)
    kv_rows = kv.shape[0] // spots
    kvo[:, :kv_rows] = kv.reshape(spots, kv_rows, wide)
    out_rows = wo.shape[0] // spots
    for j in range(grad.shape[1] // wide):
        term = dot_tn(heads[...], grad[:, j * wide : (j + 1) * wide]).astype(bf16)
        kvo[:, kv_rows + j * out_rows : kv_rows + (j + 1) * out_rows] = term.reshape(spots, out_rows, wide)
    together(prevs)
    sems.finish()


def attend_back(grad, wo, heads, q, packed, keys_all, segs, lse, kv_proj, moe_part, residual, cosine, sine):
    whole = pl.BlockSpec(memory_space=VM)
    held = pl.BlockSpec(memory_space=pl.ANY)
    rows, keys = q.shape[0], packed.shape[0]
    own_rows, width = residual.shape
    spots = lax.axis_size("seq")
    kvo_rows = (kv_proj.shape[0] * kv_proj.shape[1] + wo.shape[0] * wo.shape[1]) // spots // LAT
    return pl.pallas_call(
        attend_back_kernel,
        out_shape=[
            jax.ShapeDtypeStruct(q.shape, bf16),
            jax.ShapeDtypeStruct((rows, SPAN), bf16),
            jax.ShapeDtypeStruct((own_rows, SPAN), bf16),
            jax.ShapeDtypeStruct((spots, kvo_rows, LAT), bf16),
            jax.ShapeDtypeStruct((own_rows, width), bf16),
        ],
        in_specs=[whole] + [held] * 12,
        out_specs=[whole] * 5,
        scratch_shapes=[
            pltpu.VMEM((rows, SPAN), bf16),
            pltpu.VMEM((rows, 2 * VDIM), bf16),
            pltpu.VMEM((keys, 2 * NOPE), f32),
            pltpu.VMEM((keys, VDIM), f32),
            pltpu.VMEM((keys, 2 * ROPE), f32),
            pltpu.VMEM(packed.shape, bf16),
            pltpu.VMEM((2, rows, 2 * NOPE), f32),
            pltpu.VMEM((rows, 2 * ROPE), f32),
            pltpu.VMEM((rows, 2 * ROPE), f32),
            *(
                pltpu.VMEM(x.shape, x.dtype)
                for x in (wo, grad, moe_part, packed, keys_all, q, heads, lse, residual, kv_proj)
            ),
            *scatter_scratch(own_rows, width),
            *scatter_scratch(own_rows, SPAN),
            pltpu.SemaphoreType.DMA((20,)),
            pltpu.SemaphoreType.DMA((20,)),
            pltpu.SemaphoreType.DMA((12,)),
        ],
        compiler_params=pltpu.CompilerParams(collective_id=4, has_side_effects=True, vmem_limit_bytes=60 << 20),
        name="attend_back",
    )(segs, wo, grad, moe_part, packed, keys_all, q, heads, lse, residual, kv_proj, cosine, sine)


SEQ_TURNS = (1, 2, 3, 4, 5, 6)


def tail_kernel(
    dq, key_own, prev_out, kvo, raw, latent_gain, gain, router_in, ffn_in,
    normed_h, wq_h, wl_h, upstream_h, rows_h, cosine_h, sine_h,
    query_out, kvo_out, latent_out, grad_out, small_out,
    work0, work1, own_sum, in_part, in_sum, in_own, lat_rows, lat_all, lat_work, lat_sum, prev_in, small,
    r0, r1, r2, s0, s1, s2, k0, k1, k2, n0, n1, n2, lw, ln,
    normed, wq, wl, upstream, rows_in, cosine, sine, send, recv, local,
):
    at = Place()
    sems = Sems(send, recv)
    rows = raw.shape[0]
    half = rows // 2
    own = pl.ds(pl.multiple_of(at.me * rows, rows), rows)
    spot = pl.ds(pl.multiple_of(lax.rem(at.y, 2) * 8 * rows + at.me * rows, rows), rows)
    sources = (
        (normed_h, normed), (wq_h, wq), (wl_h, wl), (cosine_h.at[spot], cosine), (sine_h.at[spot], sine),
        (upstream_h, upstream), (rows_h, rows_in),
    )
    loads = [pltpu.make_async_copy(src, dst, local.at[2 + i]) for i, (src, dst) in enumerate(sources)]
    for c in loads:
        c.start()
    greet([at.sibling] + [at.hop(axis, d) for axis in range(3) for d in (1, 2, 3)])

    def keep_own(h, total):
        own_sum[h * half : (h + 1) * half] = total

    def keep_in(h, total):
        in_sum[h * half : (h + 1) * half] = total

    swap = sems.start(prev_out, prev_in, at.across[1](at.y + 1 - 2 * lax.rem(at.y, 2)))
    owns = scatter_stream(sems, at, key_own, k0, k1, k2, rows, keep_own)
    next(owns)
    work1[...] = kvo[...]
    second = seq_stream(sems, at, work1, kvo_out, (s0, s1, s2), (2, 1))
    next(second)
    next(owns)
    next(owns)
    loads[0].wait()
    work0[...] = dot_tn(normed[...], dq[...]).astype(bf16).reshape(work0.shape)
    first = seq_stream(sems, at, work0, query_out, (r0, r1, r2), (1, 2))
    next(first)
    next(owns)
    loads[1].wait()
    gain_part = jnp.zeros((1, normed.shape[1]), f32)
    step = 256
    for i in range(dq.shape[0] // step):
        r = pl.ds(i * step, step)
        part = dot_nt(dq[r], wq[...])
        gain_part = gain_part + jnp.sum(part * normed[r].astype(f32), axis=0, keepdims=True)
        in_part[r] = part.astype(bf16)
    in_rows = scatter_stream(sems, at, in_part, n0, n1, n2, rows, keep_in)
    running = []

    def latents():
        together(owns)
        swap.wait_recv()
        own_grad = own_sum[...] + jnp.where(lax.rem(at.y, 2) == 0, prev_in[...].astype(f32), 0.0)
        x = raw[...]
        inverse = lax.rsqrt(jnp.mean(x * x, axis=1, keepdims=True) + EPSILON)
        u = own_grad[:, :LAT]
        lat_gain_part = jnp.sum(u * x * inverse, axis=0, keepdims=True)
        s = u * latent_gain[...]
        inner = jnp.mean(s * x, axis=1, keepdims=True)
        lat_rows[:, :LAT] = (inverse * s - x * (inverse * inverse * inverse) * inner).astype(bf16)
        rope = own_grad[:, LAT:]
        loads[3].wait()
        loads[4].wait()
        rope = rope * cosine[...] - swapped(rope) * sine[...]
        lane = lax.broadcasted_iota(jnp.int32, rope.shape, 1)
        lat_rows[:, LAT:] = jnp.where(lane < ROPE, rope, 0.0).astype(bf16)
        gathered = gather_stream(sems, at, lat_rows, lat_all, rows, local.at[0])
        next(gathered)
        running.append(in_rows)
        loads[2].wait()
        in_own[...] = dot_nn(lat_rows[:, : LAT + ROPE], wl[...])
        attn_gain = gain_part + jnp.sum(in_own[...] * normed[own].astype(f32), axis=0, keepdims=True)
        small_out[:EXPERTS] = router_in[...]
        small_out[EXPERTS:] = jnp.zeros_like(router_in)
        small_out[EXPERTS : EXPERTS + 1] = attn_gain / gain[...]
        small_out[EXPERTS + 1 : EXPERTS + 2] = ffn_in[...]
        small_out[EXPERTS + 2 : EXPERTS + 3, :LAT] = lat_gain_part
        running.append(small_stream(sems, at, small, small_out))
        yield from gathered
        width = lat_work.shape[0] * lat_work.shape[1]
        mine = normed[:, pl.ds(pl.multiple_of(at.me * width, width), width)]
        lat_work[...] = dot_tn(mine, lat_all[...]).astype(bf16).reshape(lat_work.shape)
        yield from seq_direct(sems, at, lat_work, lat_sum, lw, ln)
        yield from gather_stream(sems, at, lat_sum, latent_out, lat_sum.shape[0], local.at[1])

    chain = latents()
    running.append(chain)
    count = 0
    while running:
        for stream in list(running):
            try:
                next(stream)
            except StopIteration:
                running.remove(stream)
        count += 1
        if count in SEQ_TURNS:
            next(first, None)
            next(second, None)
    together(first, second)
    loads[5].wait()
    loads[6].wait()
    u = in_sum[...] + in_own[...]
    x = rows_in[...].astype(f32)
    inverse = lax.rsqrt(jnp.mean(x * x, axis=1, keepdims=True) + EPSILON)
    s = u * gain[...]
    inner = jnp.mean(s * x, axis=1, keepdims=True)
    grad_out[...] = (upstream[...] + (inverse * s - x * (inverse * inverse * inverse) * inner)).astype(bf16)
    sems.finish()


def tail(dq, key_own, prev_out, kvo, normed, wq, wl, raw, latent_gain, gain, upstream, rows_in, router_in, ffn_in, cosine, sine):
    whole = pl.BlockSpec(memory_space=VM)
    rows, width = rows_in.shape
    spots = kvo.shape[0]
    query_shape = (spots, width // spots, dq.shape[1])
    slice_rows = width // lax.axis_size("exp") // spots
    lat_shape = (spots, slice_rows, SPAN)
    return pl.pallas_call(
        tail_kernel,
        out_shape=[
            jax.ShapeDtypeStruct(query_shape, bf16),
            jax.ShapeDtypeStruct(kvo.shape, bf16),
            jax.ShapeDtypeStruct((8 * spots, slice_rows, SPAN), bf16),
            jax.ShapeDtypeStruct((rows, width), bf16),
            jax.ShapeDtypeStruct((2 * EXPERTS, width), f32),
        ],
        in_specs=[whole] * 9 + [pl.BlockSpec(memory_space=pl.ANY)] * 7,
        out_specs=[whole] * 5,
        scratch_shapes=[
            pltpu.VMEM(query_shape, bf16),
            pltpu.VMEM(kvo.shape, bf16),
            pltpu.VMEM((rows, SPAN), f32),
            pltpu.VMEM((8 * rows, width), bf16),
            pltpu.VMEM((rows, width), f32),
            pltpu.VMEM((rows, width), f32),
            pltpu.VMEM((rows, SPAN), bf16),
            pltpu.VMEM((8 * rows, SPAN), bf16),
            pltpu.VMEM(lat_shape, bf16),
            pltpu.VMEM(lat_shape, bf16),
            pltpu.VMEM((rows, SPAN), bf16),
            pltpu.VMEM((4, 4, 2 * EXPERTS, width), bf16),
            *seq_scratch(*query_shape[1:]),
            *seq_scratch(*kvo.shape[1:]),
            *scatter_scratch(rows, SPAN),
            *scatter_scratch(rows, width),
            pltpu.VMEM((3, 4, slice_rows, SPAN), bf16),
            pltpu.VMEM((3, slice_rows, SPAN), bf16),
            pltpu.VMEM(normed.shape, bf16),
            pltpu.VMEM(wq.shape, bf16),
            pltpu.VMEM(wl.shape, bf16),
            pltpu.VMEM(upstream.shape, f32),
            pltpu.VMEM(rows_in.shape, bf16),
            pltpu.VMEM((rows, 2 * ROPE), f32),
            pltpu.VMEM((rows, 2 * ROPE), f32),
            pltpu.SemaphoreType.DMA((130,)),
            pltpu.SemaphoreType.DMA((130,)),
            pltpu.SemaphoreType.DMA((9,)),
        ],
        compiler_params=pltpu.CompilerParams(collective_id=3, has_side_effects=True, vmem_limit_bytes=60 << 20),
        name="tail",
    )(dq, key_own, prev_out, kvo, raw, latent_gain, gain, router_in, ffn_in, normed, wq, wl, upstream, rows_in, cosine, sine)


def start_kernel(
    rows_in, gain, latent_gain, routes, segs, ffn_gain, own_grad, wl_h, wq_h, kv_proj_h, wo_h, cosine_h, sine_h,
    normed_h, q_h, packed_h, keys_h, grad_h, hot_all, raw, heads, lse, residual, own_mid,
    normed, q, packed, keys, grad_half, wl, wq, kv_proj, wo,
    own_normed, ext, ext_all, prev_out, cosine, sine, part, column, p0, p1, p2, send, recv, local, load, store,
):
    at = Place()
    sems = Sems(send, recv)
    rows = rows_in.shape[0]
    block = 8 * rows
    half_seq = pl.ds(pl.multiple_of(lax.rem(at.y, 2) * block, block), block)
    sources = (
        (wl_h, wl), (cosine_h.at[half_seq], cosine), (sine_h.at[half_seq], sine), (wq_h, wq), (kv_proj_h, kv_proj), (wo_h, wo),
    )
    loads = [pltpu.make_async_copy(src, dst, load.at[i]) for i, (src, dst) in enumerate(sources)]
    for c in loads:
        c.start()
    partner = at.across[1](at.y + 1 - 2 * lax.rem(at.y, 2))
    count = announce([at.hop(0, 1), at.hop(0, 3), at.sibling, partner])
    x = rows_in[...].astype(f32)
    own_normed[...] = (x * lax.rsqrt(jnp.mean(x * x, axis=1, keepdims=True) + EPSILON) * gain[...]).astype(bf16)
    meet(count)
    big = gather_stream(sems, at, own_normed, normed, rows, local.at[0])
    next(big)
    loads[0].wait()
    lat = dot_nt(own_normed[...], wl[...])
    raw[...] = lat[:, :LAT]
    x = lat[:, :LAT]
    x = x * lax.rsqrt(jnp.mean(x * x, axis=1, keepdims=True) + EPSILON) * latent_gain[...]
    rope = jnp.concatenate([lat[:, LAT:], lat[:, LAT:]], axis=1)
    loads[1].wait()
    loads[2].wait()
    own = pl.ds(pl.multiple_of(at.me * rows, rows), rows)
    rope = rope * cosine[own] + swapped(rope) * sine[own]
    number = lax.broadcasted_iota(jnp.int32, (128, rows), 0)
    hot = jnp.zeros((128, rows), f32)
    for k in range(routes.shape[0]):
        hot = hot + jnp.where(number == routes[k : k + 1], 1.0, 0.0)
    hot = pltpu.roll(jnp.transpose(hot), ROPE, 1)
    lane = lax.broadcasted_iota(jnp.int32, rope.shape, 1)
    prev_out[:, :LAT] = x.astype(bf16)
    prev_out[:, LAT:] = jnp.where(lane < ROPE, rope, hot).astype(bf16)
    swap = sems.start(prev_out, ext.at[:, pl.ds(SPAN, SPAN)], partner)
    ext[:, :SPAN] = prev_out[...]
    next(big)
    swap.wait_recv()
    little = gather_stream(sems, at, ext, ext_all, rows, local.at[1])
    next(little)
    together(big)
    stores = [pltpu.make_async_copy(normed, normed_h, store.at[0])]
    stores[0].start()
    loads[3].wait()
    loads[4].wait()
    step = 256
    lane = lax.broadcasted_iota(jnp.int32, (step, 2 * ROPE), 1)
    for i in range(block // step):
        r = pl.ds(i * step, step)
        query = dot_nn(normed[r], wq[...])
        q[r, :NOPE] = query[:, :NOPE].astype(bf16)
        one, two = query[:, NOPE : 2 * NOPE], query[:, 2 * NOPE :]
        q[r, NOPE : 2 * NOPE] = jnp.where(lane < ROPE, pltpu.roll(one, ROPE, 1), pltpu.roll(two, ROPE, 1)).astype(bf16)
        rope = jnp.where(lane < ROPE, one, two)
        q[r, 2 * NOPE :] = (rope * cosine[r] + swapped(rope) * sine[r]).astype(bf16)
        if i % 2:
            next(little, None)
    stores.append(pltpu.make_async_copy(q, q_h, store.at[1]))
    stores[1].start()
    together(little)
    early = gather_stream(sems, at, own_grad.at[pl.ds(0, rows // 2)], grad_half, rows // 2, local.at[2])
    next(early)
    for side in range(2):
        r = pl.ds((1 - side) * block, block)
        keys[r, :LAT] = ext_all[:, side * SPAN : side * SPAN + LAT]
        rope = ext_all[:, side * SPAN + LAT : (side + 1) * SPAN].astype(f32)
        turned = pltpu.roll(rope, ROPE, 1)
        if side == 0:
            hot_all[...] = turned.astype(bf16)
        wide_lane = lax.broadcasted_iota(jnp.int32, rope.shape, 1)
        keys[r, LAT:] = jnp.where(wide_lane < ROPE, rope, turned).astype(bf16)
        packed[r] = dot_nn(ext_all[:, side * SPAN : side * SPAN + LAT], kv_proj[...]).astype(bf16)
        for ref, dst in ((keys, keys_h), (packed, packed_h)):
            stores.append(pltpu.make_async_copy(ref.at[r], dst.at[r], store.at[len(stores)]))
            stores[-1].start()
    qseg, kseg = segments(segs, block)
    column[...] = qseg
    shape = (ATT, 2 * block)
    ahead = lax.broadcasted_iota(jnp.int32, shape, 1) - lax.broadcasted_iota(jnp.int32, shape, 0)
    loads[5].wait()

    def ready(dist):
        index = lax.rem(at.chip + dist, 4)
        r = row_block(index)
        allowed = (column[r] == kseg) & (ahead <= index * ATT + block)
        for head in range(2):
            rope = jnp.where(lane // ROPE == head, q[r, 2 * NOPE :], jnp.zeros((), bf16))
            query = jnp.concatenate([q[r, head * NOPE : (head + 1) * NOPE], rope], axis=1)
            head_keys = jnp.concatenate([packed[:, head * 2 * NOPE : head * 2 * NOPE + NOPE], keys[:, LAT:]], axis=1)
            scores = jnp.where(allowed, dot_nt(query, head_keys), -1e30)
            top = jnp.max(scores, axis=1, keepdims=True)
            weights = jnp.exp2((scores - top) * (SCALE * LOG2E))
            total = jnp.sum(weights, axis=1, keepdims=True)
            out = dot_nn(weights.astype(bf16), packed[:, head * 2 * NOPE + NOPE : (head + 1) * 2 * NOPE])
            heads[r, head * VDIM : (head + 1) * VDIM] = (out / total).astype(bf16)
            lse[head, r] = top * (SCALE * LOG2E) + jnp.log2(total)
        part[r] = dot_nn(heads[r], wo[...]).astype(bf16)

    def done(h, total):
        r = slice(h * (rows // 2), (h + 1) * (rows // 2))
        x = rows_in[r].astype(f32) + total
        residual[r] = x
        own_mid[r] = (x * lax.rsqrt(jnp.mean(x * x, axis=1, keepdims=True) + EPSILON) * ffn_gain[...]).astype(bf16)

    out_rows = scatter_stream(sems, at, part, p0, p1, p2, rows, done, ready)
    next(out_rows)
    next(early)
    next(out_rows)
    next(early)
    next(out_rows)
    together(early)
    stores.append(pltpu.make_async_copy(grad_half, grad_h, store.at[len(stores)]))
    stores[-1].start()
    together(out_rows)
    for c in stores:
        c.wait()
    sems.finish()


def start(rows_in, gain, wl, latent_gain, wq, kv_proj, routes, cosine, sine, segs, wo, ffn_gain, own_grad):
    whole = pl.BlockSpec(memory_space=VM)
    held = pl.BlockSpec(memory_space=pl.ANY)
    rows, width = rows_in.shape
    block = 8 * rows
    shapes = [
        (block, width), (block, wq.shape[1]), (2 * block, kv_proj.shape[1]), (2 * block, SPAN), (block // 2, width),
    ]
    return pl.pallas_call(
        start_kernel,
        out_shape=[jax.ShapeDtypeStruct(shape, bf16) for shape in shapes]
        + [
            jax.ShapeDtypeStruct((block, 2 * ROPE), bf16),
            jax.ShapeDtypeStruct((rows, LAT), f32),
            jax.ShapeDtypeStruct((block, 2 * VDIM), bf16),
            jax.ShapeDtypeStruct((2, block, 1), f32),
            jax.ShapeDtypeStruct((rows, width), f32),
            jax.ShapeDtypeStruct((rows, width), bf16),
        ],
        in_specs=[whole] * 7 + [held] * 6,
        out_specs=[held] * 5 + [whole] * 6,
        scratch_shapes=[pltpu.VMEM(shape, bf16) for shape in shapes]
        + [pltpu.VMEM(x.shape, bf16) for x in (wl, wq, kv_proj, wo)]
        + [
            pltpu.VMEM((rows, width), bf16),
            pltpu.VMEM((rows, 2 * SPAN), bf16),
            pltpu.VMEM((block, 2 * SPAN), bf16),
            pltpu.VMEM((rows, SPAN), bf16),
            pltpu.VMEM((block, 2 * ROPE), f32),
            pltpu.VMEM((block, 2 * ROPE), f32),
            pltpu.VMEM((block, width), bf16),
            pltpu.VMEM((block, 1), f32),
            *scatter_scratch(rows, width),
            pltpu.SemaphoreType.DMA((50,)),
            pltpu.SemaphoreType.DMA((50,)),
            pltpu.SemaphoreType.DMA((3,)),
            pltpu.SemaphoreType.DMA((6,)),
            pltpu.SemaphoreType.DMA((7,)),
        ],
        compiler_params=pltpu.CompilerParams(collective_id=0, has_side_effects=True, vmem_limit_bytes=60 << 20),
        name="start",
    )(rows_in, gain, latent_gain, routes, segs, ffn_gain, own_grad, wl, wq, kv_proj, wo, cosine, sine)


def finish_kernel(
    weights_h, query_h, kvo_h, latent_h, small, early,
    expert_gate_h, expert_down_h, shared_gate_h, shared_down_h, query_out_h, kv_out_h, out_out_h, latent_out_h,
    router_out, attn_out, ffn_out, lat_gain_out,
    weights, query, kvo, latent, expert_gate, expert_down, shared_gate, shared_down, query_out, kv_out, out_out, latent_out,
    load, store,
):
    pairs = ((latent_h, latent), (query_h, query), (kvo_h, kvo), (weights_h, weights))
    loads = [pltpu.make_async_copy(src, dst, load.at[i]) for i, (src, dst) in enumerate(pairs)]
    for c in loads:
        c.start()
    stores = []

    def put(src, dst):
        c = pltpu.make_async_copy(src, dst, store.at[len(stores)])
        c.start()
        stores.append(c)

    router_out[...] = small[:EXPERTS]
    attn_out[...] = small[EXPERTS : EXPERTS + 1]
    ffn_out[...] = small[EXPERTS + 1 : EXPERTS + 2]
    lat_gain_out[...] = small[EXPERTS + 2 : EXPERTS + 3, :LAT]
    loads[0].wait()
    step = 512
    for i in range(latent_out.shape[1] // step):
        spot = step // latent.shape[1]
        rows = latent[i * spot : (i + 1) * spot].reshape(step, latent.shape[2]).astype(f32)
        latent_out[:, i * step : (i + 1) * step] = jnp.transpose(rows)[: latent_out.shape[0]]
    put(latent_out, latent_out_h)
    loads[1].wait()
    query_out[...] = query[...].reshape(query_out.shape).astype(f32)
    put(query_out, query_out_h)
    loads[2].wait()
    spots, _, wide = kvo.shape
    kv_rows = kv_out.shape[0] // spots
    kv_out[...] = kvo[:, :kv_rows].reshape(kv_out.shape).astype(f32)
    put(kv_out, kv_out_h)
    out_rows = out_out.shape[0] // spots
    for j in range(out_out.shape[1] // wide):
        piece = kvo[:, kv_rows + j * out_rows : kv_rows + (j + 1) * out_rows]
        out_out[:, j * wide : (j + 1) * wide] = piece.reshape(out_out.shape[0], wide).astype(f32)
    put(out_out, out_out_h)
    loads[3].wait()
    for c in range(expert_gate.shape[1] // 128):
        expert_gate[:, c * 128 : (c + 1) * 128] = weights[c * 128 : (c + 1) * 128].astype(f32)
    put(expert_gate, expert_gate_h)
    spot = expert_gate.shape[1]
    for ref, dst in ((expert_down, expert_down_h), (shared_gate, shared_gate_h), (shared_down, shared_down_h)):
        skip = 0
        if ref is expert_down:
            skip = early.shape[0]
            ref[:skip] = early[...].astype(f32)
        ref[skip:] = weights[spot : spot + ref.shape[0] - skip].astype(f32)
        put(ref, dst)
        spot += ref.shape[0] - skip
    for c in stores:
        c.wait()


def finish(weights, query, kvo, latent, small, early, shared, model_width, kv_shape, out_shape):
    whole = pl.BlockSpec(memory_space=VM)
    held = pl.BlockSpec(memory_space=pl.ANY)
    shapes = [
        (128, 2 * F), (F, 128), (2 * shared, 128), (shared, 128),
        (model_width, query.shape[2]), kv_shape, out_shape, (LAT + ROPE, model_width),
    ]
    little = [(EXPERTS, model_width), (1, model_width), (1, model_width), (1, LAT)]
    return pl.pallas_call(
        finish_kernel,
        out_shape=[jax.ShapeDtypeStruct(shape, f32) for shape in shapes + little],
        in_specs=[held] * 4 + [whole] * 2,
        out_specs=[held] * 8 + [whole] * 4,
        scratch_shapes=[pltpu.VMEM(x.shape, bf16) for x in (weights, query, kvo, latent)]
        + [pltpu.VMEM(shape, f32) for shape in shapes]
        + [pltpu.SemaphoreType.DMA((4,)), pltpu.SemaphoreType.DMA((8,))],
        compiler_params=pltpu.CompilerParams(vmem_limit_bytes=56 << 20),
        name="finish",
    )(weights, query, kvo, latent, small, early)


def tables(seq_rows):
    lane = np.arange(2 * ROPE)
    half = ROPE // 2
    frequency = np.exp((lane % half) * (-math.log(10000.0) / half))
    angles = np.arange(seq_rows)[:, None] * frequency[None, :]
    sign = np.where(lane % ROPE < half, -1.0, 1.0)
    return np.cos(angles).astype(np.float32), (np.sin(angles) * sign[None, :]).astype(np.float32)


def local(
    layer_input, attn_gain, query_proj, latent_proj, latent_gain, kv_proj, output_proj, ffn_gain, router_proj,
    shared_gate_up, shared_down, expert_gate_up, expert_down, segment_ids, expert_routes, out_grad,
):
    own_rows, model_width = layer_input.shape
    cosine, sine = tables(2 * own_rows * lax.axis_size("exp"))
    wl = latent_proj.T
    router = router_proj.T
    shared = shared_down.shape[0]
    pair_s = shared_gate_up.transpose(1, 2, 0).reshape(2 * shared, model_width)
    pair_e, down_e = expert_gate_up[0], expert_down[0]
    segs = segment_ids[None]
    attn_row, latent_row, ffn_row = attn_gain[None], latent_gain[None], ffn_gain[None]
    normed_all, q, packed, keys, grad_half, hot, latent_raw, heads, lse, residual, own_mid = start(
        layer_input, attn_row, wl, latent_row, query_proj, kv_proj, expert_routes.T, cosine, sine,
        segs, output_proj, ffn_row, out_grad,
    )
    terms, act, dpre, logit, router_term, early = mlp(
        own_mid, out_grad, pair_s, pair_e, shared_down, down_e, grad_half, router, hot
    )
    weight_sum = lax.psum_scatter(terms.reshape(-1, 128), "seq", scatter_dimension=0, tiled=True)
    residual_grad, ffn_term, attn_grad_all, moe_part = turn(
        dpre, act, pair_s, pair_e, shared_down, down_e, logit, router, residual, ffn_row, out_grad
    )
    dq, key_own, prev_sum, kvo, layer_output = attend_back(
        attn_grad_all, output_proj, heads, q, packed, keys, segs, lse, kv_proj, moe_part, residual, cosine, sine
    )
    query_sum, kvo_sum, latent_sum, input_grad, small = tail(
        dq, key_own, prev_sum, kvo, normed_all, query_proj, wl, latent_raw, latent_row, attn_row,
        residual_grad, layer_input, router_term, ffn_term, cosine, sine,
    )
    (
        expert_gate, expert_down_sum, shared_gate, shared_down_sum, query_sum, kv_sum, output_sum, latent_sum,
        router_sum, attn_gain_sum, ffn_gain_sum, latent_gain_sum,
    ) = finish(
        weight_sum, query_sum, kvo_sum, latent_sum, small, early, shared, model_width, kv_proj.shape, output_proj.shape
    )
    return (
        layer_output,
        input_grad,
        attn_gain_sum[0],
        query_sum,
        latent_sum.T,
        latent_gain_sum[0],
        kv_sum,
        output_sum,
        ffn_gain_sum[0],
        router_sum.T,
        shared_gate.reshape(2, shared, 128).transpose(2, 0, 1),
        shared_down_sum,
        expert_gate[None],
        expert_down_sum[None],
    )


def solution(mesh):
    in_specs = (
        P(("seq", "exp"), None),
        P(),
        P(None, "exp"),
        P(),
        P(),
        P(None, "exp"),
        P("exp", None),
        P(),
        P(),
        P(None, None, "exp"),
        P("exp", None),
        P("exp", None, None),
        P("exp", None, None),
        P(),
        P(("seq", "exp"), None),
        P(("seq", "exp"), None),
    )
    out_specs = (
        P(("seq", "exp"), None),
        P(("seq", "exp"), None),
        P(),
        P(None, "exp"),
        P(),
        P(),
        P(None, "exp"),
        P("exp", None),
        P(),
        P(),
        P("seq", None, "exp"),
        P("exp", "seq"),
        P("exp", "seq", None),
        P("exp", None, "seq"),
    )
    return jax.shard_map(local, mesh=mesh, in_specs=in_specs, out_specs=out_specs, check_vma=False)
```

profile of v0, /device:TPU:1, one launch (start us, length us, event | category | flops | bytes accessed | tf_op | source)
XLA Modules:
  0.0 363.2 jit_solution(9004429967877298369)
XLA Ops:
  7.2 0.0 reduce-scatter.2.cloned.1.call-start
  7.2 66.6 %start.1 = (bf16[1024,2048]{1,0:T(8,128)(2,1)}, bf16[1024,384]{1,0:T(8,128)(2,1)}, bf16[2048,512]{1,0:T(8,128)(2,1)}, bf16[2048,640]{1,0:T(8,128)(2,1)}, bf16[51...) custom-call(bf16[128,2048]{1,0:T(8,128)(2,1)} %rows_h.1, ...), custom_call_target="tpu_custom_call" | custom-call | tf_op jit(solution)/shard_map/start/pallas_call | solution.py:1181
  73.8 81.5 %mlp.1 = (bf16[16,4512,128]{2,1,0:T(8,128)(2,1)}, bf16[1024,1792]{1,0:T(8,128)(2,1)}, bf16[1024,3584]{1,0:T(8,128)(2,1)}, bf16[1024,128]{1,0:T(8,128)(2,1)}, f32...) custom-call(bf16[128,2048]{1,0:T(8,128)(2,1)} %get-tuple-element.57.own_mid, bf16[128,2048]{1,0:T(8,128)(2,1)} %upstream.1, ...), custom_call_target="tpu_custom_call" | custom-call | flops 44291850240 | bytes 62914560 | tf_op jit(solution)/shard_map/mlp/pallas_call | solution.py:544
  155.3 0.0 reduce-scatter.2.cloned.1.call-update
  155.4 62.2 %turn.1 = (f32[128,2048]{1,0:T(8,128)}, f32[1,2048]{1,0:T(1,128)}, bf16[1024,2048]{1,0:T(8,128)(2,1)}, bf16[1024,2048]{1,0:T(8,128)(2,1)}) custom-call(bf16[1024,3584]{1,0:T(8,128)(2,1)} %get-tuple-element.60.dpre_h, bf16[1024,1792]{1,0:T(8,128)(2,1)} %get-tuple-element.61.act_h, bf16[704,2048]{1,0:T(8,128)(2,1)} %bitcast.31, bf16[2048,2816]{1,0:T(8,128)(2,1)} %bitcast.25, ...), custom_call_target="tpu_custom_call" | custom-call | tf_op jit(solution)/shard_map/turn/pallas_call | solution.py:663
  217.5 37.0 %attend_back.1 = (bf16[1024,384]{1,0:T(8,128)(2,1)}, bf16[1024,640]{1,0:T(8,128)(2,1)}, bf16[128,640]{1,0:T(8,128)(2,1)}, bf16[16,96,512]{2,1,0:T(8,128)(2,1)}, bf16[128,2048]{1,0:T(8,128)(2,1)}) custom-call(s32[1,16384]{1,0:T(1,128)} %bitcast.33, bf16[256,2048]{1,0:T(8,128)(2,1)} %wo_h.3, bf16[1024,2048]{1,0:T(8,128)(2,1)} %get-tuple-element.64.grad_h, ...), custom_call_target="tpu_custom_call" | custom-call | tf_op jit(solution)/shard_map/attend_back/pallas_call | solution.py:840
  254.6 90.4 %tail.1 = (bf16[16,128,384]{2,1,0:T(8,128)(2,1)}, bf16[16,96,512]{2,1,0:T(8,128)(2,1)}, bf16[128,16,640]{2,1,0:T(8,128)(2,1)}, bf16[128,2048]{1,0:T(8,128)(2,1)}, f32[16,2048]{1,0:T(8,128)}) custom-call(bf16[1024,384]{1,0:T(8,128)(2,1)} %get-tuple-element.72.dq, bf16[1024,640]{1,0:T(8,128)(2,1)} %get-tuple-element.73.key_own, ...), custom_call_target="tpu_custom_call" | custom-call | tf_op jit(solution)/shard_map/tail/pallas_call | solution.py:1000
  345.0 0.0 reduce-scatter.2.cloned.1.call-done.weights_h
  345.0 0.0 copy-start
  345.0 0.0 copy-start.1
  345.1 9.2 %finish.1 = (f32[128,2816]{1,0:T(8,128)}, f32[1408,128]{1,0:T(8,128)}, f32[704,128]{1,0:T(8,128)}, f32[352,128]{1,0:T(8,128)}, f32[2048,384]{1,0:T(8,128)}, /*in...) custom-call(bf16[4512,128]{1,0:T(8,128)(2,1)} %reduce-scatter.2.clon, ...), custom_call_target="tpu_custom_call" | custom-call | tf_op jit(solution)/shard_map/finish/pallas_call | solution.py:1284
  354.3 0.0 copy-done
  354.3 0.8 copy.34
  355.1 0.0 copy-done.1
  355.1 0.8 copy.35
Async XLA Ops:
  7.2 337.9 %reduce-scatter.2.cloned.1.call-start = ((), (), s32[]{:S(2)}) async-start(), calls=%async_computation.1 | async-start | bytes 19636224 | tf_op jit(solution)/shard_map/reduce_scatter | solution.py:1326
  345.0 9.3 %copy-start = (bf16[128,2048]{1,0:T(8,128)(2,1)S(1)}, bf16[128,2048]{1,0:T(8,128)(2,1)}, u32[]{:S(2)}) copy-start(bf16[128,2048]{1,0:T(8,128)(2,1)} %get-tuple-element.114) | copy-start | bytes 1572868
  345.0 10.1 %copy-start.1 = (bf16[128,2048]{1,0:T(8,128)(2,1)S(1)}, bf16[128,2048]{1,0:T(8,128)(2,1)}, u32[]{:S(2)}) copy-start(bf16[128,2048]{1,0:T(8,128)(2,1)} %get-tuple-element.115) | copy-start | bytes 1572868
Sparse Core Ops, SparseCore 0:
  155.5 126.3 reduce-scatter.1
where the time goes:
time: 367 us; the launch traced here: 363 us
  Pallas kernels  347 us (95%)
  between operations  14.6 us (4%)
    pallas_call x1, Pallas kernels, tail(): pl.pallas_call(tail_kernel, out_shape=[jax.ShapeDtypeStruct(query_shape,...  90.4 us
    pallas_call x1, Pallas kernels, mlp(): pl.pallas_call(mlp_kernel, out_shape=[jax.ShapeDtypeStruct((width // 128,...  81.5 us
    pallas_call x1, Pallas kernels, start(): pl.pallas_call(start_kernel, out_shape=[jax.ShapeDtypeStruct(shape, bf16)...  66.6 us
    pallas_call x1, Pallas kernels, turn(): pl.pallas_call(turn_kernel, out_shape=[jax.ShapeDtypeStruct((rows, width)...  62.2 us
    pallas_call x1, Pallas kernels, attend_back(): pl.pallas_call(attend_back_kernel, out_shape=[jax.ShapeDtypeStruct(q.shap...  37 us
    pallas_call x1, Pallas kernels, finish(): pl.pallas_call(finish_kernel, out_shape=[jax.ShapeDtypeStruct(shape, f32)...  9.23 us
  transfers between devices with their start and end apart: 1, of which 0 were waited for; matrix products, arithmetic and copies ran while one was open for 0% of the time, Pallas kernels for 52%

commit v1 on v0

--- a/solution.py
+++ b/solution.py
@@ -877,9 +877,10 @@
 
 
 def tail_kernel(
-    dq, key_own, prev_out, kvo, raw, latent_gain, gain, router_in, ffn_in,
-    normed_h, wq_h, wl_h, upstream_h, rows_h, cosine_h, sine_h,
-    query_out, kvo_out, latent_out, grad_out, small_out,
+    key_own, prev_out, raw, latent_gain, gain, router_in, ffn_in,
+    kvo_h, dq_h, normed_h, wq_h, wl_h, upstream_h, rows_h, cosine_h, sine_h,
+    query_h, kvo_out_h, latent_out, grad_out, small_out,
+    query_out, kvo_out, dq,
     work0, work1, own_sum, in_part, in_sum, in_own, lat_rows, lat_all, lat_work, lat_sum, prev_in, small,
     r0, r1, r2, s0, s1, s2, k0, k1, k2, n0, n1, n2, lw, ln,
     normed, wq, wl, upstream, rows_in, cosine, sine, send, recv, local,
@@ -892,11 +893,11 @@
     spot = pl.ds(pl.multiple_of(lax.rem(at.y, 2) * 8 * rows + at.me * rows, rows), rows)
     sources = (
         (normed_h, normed), (wq_h, wq), (wl_h, wl), (cosine_h.at[spot], cosine), (sine_h.at[spot], sine),
-        (upstream_h, upstream), (rows_h, rows_in),
+        (upstream_h, upstream), (rows_h, rows_in), (kvo_h, work1), (dq_h, dq),
     )
-    loads = [pltpu.make_async_copy(src, dst, local.at[2 + i]) for i, (src, dst) in enumerate(sources)]
-    for c in loads:
-        c.start()
+    loads = [pltpu.make_async_copy(src, dst, local.at[4 + i]) for i, (src, dst) in enumerate(sources)]
+    for i in (7, 8, 0, 1, 2, 3, 4, 5, 6):
+        loads[i].start()
     greet([at.sibling] + [at.hop(axis, d) for axis in range(3) for d in (1, 2, 3)])
 
     def keep_own(h, total):
@@ -908,14 +909,21 @@
     swap = sems.start(prev_out, prev_in, at.across[1](at.y + 1 - 2 * lax.rem(at.y, 2)))
     owns = scatter_stream(sems, at, key_own, k0, k1, k2, rows, keep_own)
     next(owns)
-    work1[...] = kvo[...]
-    second = seq_stream(sems, at, work1, kvo_out, (s0, s1, s2), (2, 1))
+    keeps = [pltpu.make_async_copy(query_out, query_h, local.at[2]), pltpu.make_async_copy(kvo_out, kvo_out_h, local.at[3])]
+
+    def kept(stream, copy):
+        yield from stream
+        copy.start()
+
+    loads[7].wait()
+    second = kept(seq_stream(sems, at, work1, kvo_out, (s0, s1, s2), (2, 1)), keeps[1])
     next(second)
     next(owns)
     next(owns)
     loads[0].wait()
+    loads[8].wait()
     work0[...] = dot_tn(normed[...], dq[...]).astype(bf16).reshape(work0.shape)
-    first = seq_stream(sems, at, work0, query_out, (r0, r1, r2), (1, 2))
+    first = kept(seq_stream(sems, at, work0, query_out, (r0, r1, r2), (1, 2)), keeps[0])
     next(first)
     next(owns)
     loads[1].wait()
@@ -987,11 +995,14 @@
     s = u * gain[...]
     inner = jnp.mean(s * x, axis=1, keepdims=True)
     grad_out[...] = (upstream[...] + (inverse * s - x * (inverse * inverse * inverse) * inner)).astype(bf16)
+    for c in keeps:
+        c.wait()
     sems.finish()
 
 
 def tail(dq, key_own, prev_out, kvo, normed, wq, wl, raw, latent_gain, gain, upstream, rows_in, router_in, ffn_in, cosine, sine):
     whole = pl.BlockSpec(memory_space=VM)
+    held = pl.BlockSpec(memory_space=pl.ANY)
     rows, width = rows_in.shape
     spots = kvo.shape[0]
     query_shape = (spots, width // spots, dq.shape[1])
@@ -1006,9 +1017,12 @@
             jax.ShapeDtypeStruct((rows, width), bf16),
             jax.ShapeDtypeStruct((2 * EXPERTS, width), f32),
         ],
-        in_specs=[whole] * 9 + [pl.BlockSpec(memory_space=pl.ANY)] * 7,
-        out_specs=[whole] * 5,
+        in_specs=[whole] * 7 + [held] * 9,
+        out_specs=[held] * 2 + [whole] * 3,
         scratch_shapes=[
+            pltpu.VMEM(query_shape, bf16),
+            pltpu.VMEM(kvo.shape, bf16),
+            pltpu.VMEM(dq.shape, bf16),
             pltpu.VMEM(query_shape, bf16),
             pltpu.VMEM(kvo.shape, bf16),
             pltpu.VMEM((rows, SPAN), f32),
@@ -1036,11 +1050,11 @@
             pltpu.VMEM((rows, 2 * ROPE), f32),
             pltpu.SemaphoreType.DMA((130,)),
             pltpu.SemaphoreType.DMA((130,)),
-            pltpu.SemaphoreType.DMA((9,)),
+            pltpu.SemaphoreType.DMA((13,)),
         ],
         compiler_params=pltpu.CompilerParams(collective_id=3, has_side_effects=True, vmem_limit_bytes=60 << 20),
         name="tail",
-    )(dq, key_own, prev_out, kvo, raw, latent_gain, gain, router_in, ffn_in, normed, wq, wl, upstream, rows_in, cosine, sine)
+    )(key_own, prev_out, raw, latent_gain, gain, router_in, ffn_in, kvo, dq, normed, wq, wl, upstream, rows_in, cosine, sine)
 
 
 def start_kernel(
@@ -1215,13 +1229,13 @@
 
 
 def finish_kernel(
-    weights_h, query_h, kvo_h, latent_h, small, early,
+    weights_h, query_h, kvo_h, latent_h, layer_h, grad_h, small, early,
     expert_gate_h, expert_down_h, shared_gate_h, shared_down_h, query_out_h, kv_out_h, out_out_h, latent_out_h,
-    router_out, attn_out, ffn_out, lat_gain_out,
+    layer_out_h, grad_out_h, router_out, attn_out, ffn_out, lat_gain_out,
     weights, query, kvo, latent, expert_gate, expert_down, shared_gate, shared_down, query_out, kv_out, out_out, latent_out,
     load, store,
 ):
-    pairs = ((latent_h, latent), (query_h, query), (kvo_h, kvo), (weights_h, weights))
+    pairs = ((query_h, query), (latent_h, latent), (kvo_h, kvo), (weights_h, weights))
     loads = [pltpu.make_async_copy(src, dst, load.at[i]) for i, (src, dst) in enumerate(pairs)]
     for c in loads:
         c.start()
@@ -1232,20 +1246,22 @@
         c.start()
         stores.append(c)
 
+    put(layer_h, layer_out_h)
+    put(grad_h, grad_out_h)
     router_out[...] = small[:EXPERTS]
     attn_out[...] = small[EXPERTS : EXPERTS + 1]
     ffn_out[...] = small[EXPERTS + 1 : EXPERTS + 2]
     lat_gain_out[...] = small[EXPERTS + 2 : EXPERTS + 3, :LAT]
     loads[0].wait()
+    query_out[...] = query[...].reshape(query_out.shape).astype(f32)
+    put(query_out, query_out_h)
+    loads[1].wait()
     step = 512
     for i in range(latent_out.shape[1] // step):
         spot = step // latent.shape[1]
         rows = latent[i * spot : (i + 1) * spot].reshape(step, latent.shape[2]).astype(f32)
         latent_out[:, i * step : (i + 1) * step] = jnp.transpose(rows)[: latent_out.shape[0]]
-    put(latent_out, latent_out_h)
-    loads[1].wait()
-    query_out[...] = query[...].reshape(query_out.shape).astype(f32)
-    put(query_out, query_out_h)
+        put(latent_out.at[:, pl.ds(i * step, step)], latent_out_h.at[:, pl.ds(i * step, step)])
     loads[2].wait()
     spots, _, wide = kvo.shape
     kv_rows = kv_out.shape[0] // spots
@@ -1273,7 +1289,7 @@
         c.wait()
 
 
-def finish(weights, query, kvo, latent, small, early, shared, model_width, kv_shape, out_shape):
+def finish(weights, query, kvo, latent, layer_output, input_grad, small, early, shared, model_width, kv_shape, out_shape):
     whole = pl.BlockSpec(memory_space=VM)
     held = pl.BlockSpec(memory_space=pl.ANY)
     shapes = [
@@ -1283,15 +1299,17 @@
     little = [(EXPERTS, model_width), (1, model_width), (1, model_width), (1, LAT)]
     return pl.pallas_call(
         finish_kernel,
-        out_shape=[jax.ShapeDtypeStruct(shape, f32) for shape in shapes + little],
-        in_specs=[held] * 4 + [whole] * 2,
-        out_specs=[held] * 8 + [whole] * 4,
+        out_shape=[jax.ShapeDtypeStruct(shape, f32) for shape in shapes]
+        + [jax.ShapeDtypeStruct(x.shape, bf16) for x in (layer_output, input_grad)]
+        + [jax.ShapeDtypeStruct(shape, f32) for shape in little],
+        in_specs=[held] * 6 + [whole] * 2,
+        out_specs=[held] * 10 + [whole] * 4,
         scratch_shapes=[pltpu.VMEM(x.shape, bf16) for x in (weights, query, kvo, latent)]
         + [pltpu.VMEM(shape, f32) for shape in shapes]
-        + [pltpu.SemaphoreType.DMA((4,)), pltpu.SemaphoreType.DMA((8,))],
+        + [pltpu.SemaphoreType.DMA((4,)), pltpu.SemaphoreType.DMA((16,))],
         compiler_params=pltpu.CompilerParams(vmem_limit_bytes=56 << 20),
         name="finish",
-    )(weights, query, kvo, latent, small, early)
+    )(weights, query, kvo, latent, layer_output, input_grad, small, early)
 
 
 def tables(seq_rows):
@@ -1336,9 +1354,9 @@
     )
     (
         expert_gate, expert_down_sum, shared_gate, shared_down_sum, query_sum, kv_sum, output_sum, latent_sum,
-        router_sum, attn_gain_sum, ffn_gain_sum, latent_gain_sum,
+        layer_output, input_grad, router_sum, attn_gain_sum, ffn_gain_sum, latent_gain_sum,
     ) = finish(
-        weight_sum, query_sum, kvo_sum, latent_sum, small, early, shared, model_width, kv_proj.shape, output_proj.shape
+        weight_sum, query_sum, kvo_sum, latent_sum, layer_output, input_grad, small, early, shared, model_width, kv_proj.shape, output_proj.shape
     )
     return (
         layer_output,

time: 367 us -> 390 us (1.063)
  Pallas kernels: 347 us -> 371 us
    pallas_call x1, Pallas kernels: 9.23 us -> 34.7 us  [finish(): pl.pallas_call(finish_kernel, out_shape=[jax.ShapeDtypeStruct(shape, f32)...]
  transfers between devices with their start and end apart: 1 -> 1, of which waited for: 0 -> 0; matrix products, arithmetic and copies ran while one was open for 0% -> 0% of each run, Pallas kernels for 52% -> 49%
where the time goes in v1:
time: 390 us; the launch traced here: 386 us
  Pallas kernels  371 us (95%)
  between operations  14.5 us (4%)
    pallas_call x1, Pallas kernels, tail(): pl.pallas_call(tail_kernel, out_shape=[jax.ShapeDtypeStruct(query_shape,...  89.4 us
    pallas_call x1, Pallas kernels, mlp(): pl.pallas_call(mlp_kernel, out_shape=[jax.ShapeDtypeStruct((width // 128,...  81.5 us
    pallas_call x1, Pallas kernels, start(): pl.pallas_call(start_kernel, out_shape=[jax.ShapeDtypeStruct(shape, bf16)...  66.6 us
    pallas_call x1, Pallas kernels, turn(): pl.pallas_call(turn_kernel, out_shape=[jax.ShapeDtypeStruct((rows, width)...  62.2 us
    pallas_call x1, Pallas kernels, attend_back(): pl.pallas_call(attend_back_kernel, out_shape=[jax.ShapeDtypeStruct(q.shap...  37 us
    pallas_call x1, Pallas kernels, finish(): pl.pallas_call(finish_kernel, out_shape=[jax.ShapeDtypeStruct(shape, f32)...  34.7 us
  transfers between devices with their start and end apart: 1, of which 0 were waited for; matrix products, arithmetic and copies ran while one was open for 0% of the time, Pallas kernels for 49%

profile of v1, /device:TPU:1, one launch (start us, length us, event | category | flops | bytes accessed | tf_op | source)
XLA Modules:
  0.0 386.1 jit_solution(9787486144561754461)
XLA Ops:
  7.2 0.0 reduce-scatter.2.cloned.1.call-start
  7.2 66.6 %start.1 = (bf16[1024,2048]{1,0:T(8,128)(2,1)}, bf16[1024,384]{1,0:T(8,128)(2,1)}, bf16[2048,512]{1,0:T(8,128)(2,1)}, bf16[2048,640]{1,0:T(8,128)(2,1)}, bf16[51...) custom-call(bf16[128,2048]{1,0:T(8,128)(2,1)} %rows_h.1, ...), custom_call_target="tpu_custom_call" | custom-call | tf_op jit(solution)/shard_map/start/pallas_call | solution.py:1195
  73.8 81.5 %mlp.1 = (bf16[16,4512,128]{2,1,0:T(8,128)(2,1)}, bf16[1024,1792]{1,0:T(8,128)(2,1)}, bf16[1024,3584]{1,0:T(8,128)(2,1)}, bf16[1024,128]{1,0:T(8,128)(2,1)}, f32...) custom-call(bf16[128,2048]{1,0:T(8,128)(2,1)} %get-tuple-element.59.own_mid, bf16[128,2048]{1,0:T(8,128)(2,1)} %upstream.1, ...), custom_call_target="tpu_custom_call" | custom-call | flops 44291850240 | bytes 62914560 | tf_op jit(solution)/shard_map/mlp/pallas_call | solution.py:544
  155.4 0.0 reduce-scatter.2.cloned.1.call-update
  155.4 62.2 %turn.1 = (f32[128,2048]{1,0:T(8,128)}, f32[1,2048]{1,0:T(1,128)}, bf16[1024,2048]{1,0:T(8,128)(2,1)}, bf16[1024,2048]{1,0:T(8,128)(2,1)}) custom-call(bf16[1024,3584]{1,0:T(8,128)(2,1)} %get-tuple-element.63.dpre_h, bf16[1024,1792]{1,0:T(8,128)(2,1)} %get-tuple-element.64.act_h, bf16[704,2048]{1,0:T(8,128)(2,1)} %bitcast.31, bf16[2048,2816]{1,0:T(8,128)(2,1)} %bitcast.25, ...), custom_call_target="tpu_custom_call" | custom-call | tf_op jit(solution)/shard_map/turn/pallas_call | solution.py:663
  217.6 37.0 %attend_back.1 = (bf16[1024,384]{1,0:T(8,128)(2,1)}, bf16[1024,640]{1,0:T(8,128)(2,1)}, bf16[128,640]{1,0:T(8,128)(2,1)}, bf16[16,96,512]{2,1,0:T(8,128)(2,1)}, bf16[128,2048]{1,0:T(8,128)(2,1)}) custom-call(s32[1,16384]{1,0:T(1,128)} %bitcast.33, bf16[256,2048]{1,0:T(8,128)(2,1)} %wo_h.3, bf16[1024,2048]{1,0:T(8,128)(2,1)} %get-tuple-element.67.grad_h, ...), custom_call_target="tpu_custom_call" | custom-call | tf_op jit(solution)/shard_map/attend_back/pallas_call | solution.py:840
  254.6 89.4 %tail.1 = (bf16[16,128,384]{2,1,0:T(8,128)(2,1)}, bf16[16,96,512]{2,1,0:T(8,128)(2,1)}, bf16[128,16,640]{2,1,0:T(8,128)(2,1)}, bf16[128,2048]{1,0:T(8,128)(2,1)}, f32[16,2048]{1,0:T(8,128)}) custom-call(bf16[1024,640]{1,0:T(8,128)(2,1)} %get-tuple-element.74.key_own, bf16[128,640]{1,0:T(8,128)(2,1)} %get-tuple-element.75.prev_out, ...), custom_call_target="tpu_custom_call" | custom-call | tf_op jit(solution)/shard_map/tail/pallas_call | solution.py:1011
  344.1 0.0 reduce-scatter.2.cloned.1.call-done.weights_h
  344.1 34.7 %finish.1 = (f32[128,2816]{1,0:T(8,128)}, f32[1408,128]{1,0:T(8,128)}, f32[704,128]{1,0:T(8,128)}, f32[352,128]{1,0:T(8,128)}, f32[2048,384]{1,0:T(8,128)}, /*in...) custom-call(bf16[4512,128]{1,0:T(8,128)(2,1)} %reduce-scatter.2.clon, ...), custom_call_target="tpu_custom_call" | custom-call | tf_op jit(solution)/shard_map/finish/pallas_call | solution.py:1300
Async XLA Ops:
  7.2 336.9 %reduce-scatter.2.cloned.1.call-start = ((), (), s32[]{:S(2)}) async-start(), calls=%async_computation.1 | async-start | bytes 19636224 | tf_op jit(solution)/shard_map/reduce_scatter | solution.py:1344
Sparse Core Ops, SparseCore 0:
  155.5 126.8 reduce-scatter.1
